TPU v7x, 512 devices: a whole 4x8x8 slice. The times are simulated.
512 devices in a mesh: samp: 64 (over y, x, core), var: 8 (over z).
Axes of the slice: x: 4, y: 8, z: 8, core: 2. Of those that a mesh axis runs over, the one named last changes fastest.
Arguments:
- active_geno: bfloat16 [32768, 16384], P('samp', 'var'), may hold values from 0 to 2
- screen_geno: bfloat16 [32768, 16384], P('samp', 'var'), may hold values from 0 to 2
- beta: bfloat16 [16384, 32], P('var'), may hold values from -0.046875 to 0.046875
- counts: int32 [32, 32768], P(None, 'samp'), may hold values from 1 to 4
- ipcw: float32 [32768], P('samp'), may hold values from 1 to 5
- events: int32 [32768], P('samp'), may hold values 0 or 1
- order: int32 [64, 512], P('samp'), may hold values from 0 to 511, each once within a row
Outputs:
- grad_active: float32 [32, 16384], P(None, ('var', 'samp'))
- score_screen: float32 [32, 16384], P(None, ('var', 'samp'))
Inputs may be any that keep to these rules, and one draw needn't show every extreme that they name: Each row of order holds every rank 0 to 511 once; blocks come in event-time order along samp.
All inputs are finite; a program needn't handle non-finite values. No bound on the sum of `events` on one device may be relied on, other than what follows from the above.
Results may differ from a plain program's by a relative error of at most 0.005.
Values sent between devices are 32-bit elements; how exact they have to be, the bound alone decides.
A program may use at most 64 MiB of HBM per device.

v0:
```python
import jax
import jax.numpy as jnp
from jax import lax
from jax.sharding import PartitionSpec as P


def entering(array, axis, combine, identity, reverse):
    size, place = (lax.axis_size(axis), lax.axis_index(axis))
    everything = lax.all_gather(array, axis)
    start = jnp.broadcast_to(jnp.asarray(identity, array.dtype), array.shape)

    def lap(k, before):
        at = size - 1 - k if reverse else k
        reached = at > place if reverse else at < place
        new = combine(before, everything[at])
        return jnp.where(reached, new, before)

    return lax.fori_loop(0, size, lap, start)


def adding(earlier, later_part):
    return earlier + later_part


def per_device(active_geno, screen_geno, beta, counts, ipcw, events, order):
    wts = counts.astype(jnp.float32) * ipcw[None, :]
    partial_eta = lax.dot_general(
        beta, active_geno, (((0,), (1,)), ((), ())), preferred_element_type=jnp.float32
    )
    flagged = events.astype(jnp.float32)[None, :] * wts
    eta = lax.psum(partial_eta, "var")
    risk = wts * jnp.exp(eta)
    ranks = order[0]
    later = (ranks[:, None] >= ranks[None, :]).astype(jnp.float32)
    suffix_local = jnp.dot(risk, later, precision=lax.Precision.HIGHEST)
    risk_total = jnp.sum(risk, axis=1)
    zeros_boot = jnp.zeros_like(risk_total)
    blocks = lax.axis_size("samp")
    after = entering(risk_total, "samp", adding, zeros_boot, True)
    total_risk = suffix_local + after[:, None]
    haz = flagged / total_risk
    prefix_local = jnp.dot(haz, later.T, precision=lax.Precision.HIGHEST)
    haz_total = jnp.sum(haz, axis=1)
    before = entering(haz_total, "samp", adding, zeros_boot, False)
    cum = prefix_local + before[:, None]
    resid = (flagged - risk * cum).astype(jnp.bfloat16)
    scale = float(active_geno.shape[0] * blocks) ** (-0.5)
    grad_terms = (
        lax.dot_general(
            resid, active_geno, (((1,), (0,)), ((), ())), preferred_element_type=jnp.float32
        )
        * scale
    )
    score_terms = (
        lax.dot_general(
            resid, screen_geno, (((1,), (0,)), ((), ())), preferred_element_type=jnp.float32
        )
        * scale
    )
    grad_active, score_screen = (
        lax.psum_scatter(grad_terms, "samp", scatter_dimension=1, tiled=True),
        lax.psum_scatter(score_terms, "samp", scatter_dimension=1, tiled=True),
    )
    return (grad_active, score_screen)


def solution(mesh):
    placed = (
        P("samp", "var"),
        P("samp", "var"),
        P("var", None),
        P(None, "samp"),
        P("samp"),
        P("samp"),
        P("samp", None),
    )
    return jax.shard_map(
        per_device,
        mesh=mesh,
        in_specs=placed,
        out_specs=(P(None, ("var", "samp")), P(None, ("var", "samp"))),
        check_vma=False,
    )
```

profile of v0, /device:TPU:1, one launch (start us, length us, event | category | flops | bytes accessed | tf_op | source)
XLA Modules:
  0.0 655.5 jit_solution(18445350964241409712)
XLA Ops:
  7.2 0.0 copy-start
  7.2 0.0 copy-start.3
  7.2 0.0 copy-start.1
  7.2 0.0 copy-start.2
  7.2 0.0 copy-start.4
  7.2 0.0 all-reduce.4.cloned.1.call-start
  7.3 1.5 copy-done
  8.8 2.3 fusion.29
  11.0 0.0 all-reduce.4.cloned.1.call-update
  11.0 0.0 reduce-scatter.7.cloned.1.call-start
  11.1 0.0 copy-done.3
  11.2 1.3 dynamic-slice
  13.2 76.4 %all-reduce.4.cloned.1.call-done = f32[32,512]{1,0:T(8,128)} async-done(((f32[32,512]{1,0:T(8,128)}), f32[32,512]{1,0:T(8,128)}) %all-reduce.4.cloned.1.call-update) | async-done | bytes 65552 | tf_op jit(solution)/shard_map/psum | solution.py:31
  89.6 0.0 copy-done.1
  89.6 0.0 copy-done.2
  89.6 1.0 fusion.27
  90.6 0.3 dynamic-update-slice
  90.9 130.6 %all-reduce = f32[2048]{0:T(1024)S(1)} all-reduce(f32[2048]{0:T(1024)S(1)} %dynamic-update-slice), channel_id=2, replica_groups=mesh['samp'=64,'var'=8] {'samp'}, use_global_device_ids=true, to_apply=%add | all-reduce | flops 2048 | bytes 16384
  221.5 0.1 reshape.9
  221.6 3.0 while.30
  224.5 0.0 copy-done.4
  224.5 1.5 fusion.28
  226.0 0.3 dynamic-update-slice.1
  226.3 126.1 %all-reduce.1 = f32[2048]{0:T(1024)S(1)} all-reduce(f32[2048]{0:T(1024)S(1)} %dynamic-update-slice.1), channel_id=3, replica_groups=mesh['samp'=64,'var'=8] {'samp'}, use_global_device_ids=true, to_apply=%add.1 | all-reduce | flops 2048 | bytes 16384
  352.4 0.1 reshape.10
  352.5 2.6 while.31
  355.0 1.5 fusion.19
  356.6 0.5 convolution_multiply_fusion.1
  357.0 1.3 copy.9
  358.4 0.0 reduce-scatter.7.cloned.1.call-update
  358.4 0.0 reduce-scatter.9.cloned.1.call-start
  358.4 2.1 convolution_multiply_fusion
  360.5 1.4 copy.11
  361.9 0.0 reduce-scatter.9.cloned.1.call-update
  361.9 134.3 %reduce-scatter.7.cloned.1.call-done = f32[32,32]{1,0:T(8,128)} async-done(((f32[2048,32]{1,0:T(8,128)}), f32[32,32]{1,0:T(8,128)}) %reduce-scatter.7.cloned.1.call-update) | async-done | bytes 4112
  496.2 1.4 copy.10
  497.6 149.9 %reduce-scatter.9.cloned.1.call-done = f32[32,32]{1,0:T(8,128)} async-done(((f32[2048,32]{1,0:T(8,128)}), f32[32,32]{1,0:T(8,128)}) %reduce-scatter.9.cloned.1.call-update) | async-done | bytes 4112
  647.5 1.4 copy.12
  (133 shorter events, 2.2 us)
Async XLA Ops:
  7.2 1.6 copy-start
  7.2 4.0 copy-start.3
  7.2 82.4 %copy-start.1 = (s32[32,512]{1,0:T(8,128)S(1)}, s32[32,512]{1,0:T(8,128)}, u32[]{:S(2)}) copy-start(s32[32,512]{1,0:T(8,128)} %param.14) | copy-start | bytes 196612
  7.2 82.4 %copy-start.2 = (f32[512]{0:T(512)S(1)}, f32[512]{0:T(512)}, u32[]{:S(2)}) copy-start(f32[512]{0:T(512)} %param.15) | copy-start | bytes 6148
  7.2 217.3 %copy-start.4 = (s32[1,512]{1,0:T(1,128)S(1)}, s32[1,512]{1,0:T(1,128)}, u32[]{:S(2)}) copy-start(s32[1,512]{1,0:T(1,128)} %param.17) | copy-start | bytes 6148
  7.2 82.4 %all-reduce.4.cloned.1.call-start = ((), (), s32[]{:S(2)}) async-start(), calls=%async_computation.2 | async-start | bytes 131072 | tf_op jit(solution)/shard_map/psum | solution.py:31
  11.0 485.2 %reduce-scatter.7.cloned.1.call-start = ((), (), s32[]{:S(2)}) async-start(), calls=%async_computation.3 | async-start | bytes 1064960
  358.4 289.1 %reduce-scatter.9.cloned.1.call-start = ((), (), s32[]{:S(2)}) async-start(), calls=%async_computation.4 | async-start | bytes 1064960
Sparse Core Ops, SparseCore 0:
  11.2 78.3 all-reduce.3
  358.5 137.6 reduce-scatter.6
  501.5 146.0 reduce-scatter.8
where the time goes:
time: 660 us; the launch traced here: 655 us
  waiting for transfers between devices  361 us (55%)
  blocking collectives  257 us (39%)
  between operations  14.6 us (2%)
  local copies, waits for them, and re-layouts  9.08 us (1%)
  matrix products  7.77 us (1%)
    unnamed x5, waiting for transfers between devices  284 us
    unnamed x2, blocking collectives  257 us
    psum x1, waiting for transfers between devices, per_device(): eta = lax.psum(partial_eta, 'var')  76.4 us
  transfers between devices with their start and end apart: 3, of which 3 were waited for; matrix products, arithmetic and copies ran while one was open for 1% of the time, Pallas kernels for 0%

commit v1 on v0

v1 whole, which is shorter than its diff:
```python
import functools
import jax
import jax.numpy as jnp
from jax import lax
from jax.experimental import pallas as pl
from jax.experimental.pallas import tpu as pltpu
from jax.sharding import PartitionSpec as P

MESH = pl.DeviceIdType.MESH
NY, NX, NC, NZ = 8, 4, 2, 8
NG = NX * NC
HALF = 256
F32 = jnp.float32
BF16 = jnp.bfloat16


def lane_iota(shape):
    return lax.broadcasted_iota(jnp.int32, shape, 1)


def row_iota(shape):
    return lax.broadcasted_iota(jnp.int32, shape, 0)


def swap4(tile):
    return pltpu.roll(tile, 4, 0)


def fold_halves(low, high, upper):
    top = row_iota(low.shape) < 4
    even = jnp.where(top, low, swap4(high))
    odd = jnp.where(top, swap4(low), high)
    return jnp.where(upper, odd, even)


def split2(value):
    high = value.astype(BF16)
    rest = value - high.astype(F32)
    return jnp.concatenate([high.astype(F32), rest], axis=0).astype(BF16)


def masked_sums(value, mask_ref):
    pieces = split2(value)
    first = jnp.dot(pieces, mask_ref[0:HALF, :], preferred_element_type=F32)
    second = jnp.dot(pieces, mask_ref[HALF:, :], preferred_element_type=F32)
    first = first[0:8] + first[8:16]
    second = second[0:8] + second[8:16]
    top = row_iota((8, HALF)) < 4
    low = jnp.where(top, first[:, :HALF], second[:, :HALF])
    low = low + swap4(low)
    high = jnp.where(top, first[:, HALF:], second[:, HALF:])
    high = high + swap4(high)
    return jnp.where(top, low, high)


def to_lanes(value):
    total = jnp.sum(value, axis=1, keepdims=True)
    total = jnp.broadcast_to(total, (8, 128))
    total = total + swap4(total)
    lane, row = lane_iota((8, 128)), row_iota((8, 128))
    return jnp.sum(jnp.where(lane % 8 == row, total, 0.0), axis=0, keepdims=True)


def to_rows(value):
    lane, row = lane_iota((8, 128)), row_iota((8, 128))
    return jnp.sum(jnp.where(lane == row, jnp.broadcast_to(value, (8, 128)), 0.0), axis=1, keepdims=True)


def kernel(scale, active, screen, beta, counts, ipcw, events, order, grad, score,
           act_v, scr_v, beta_v, cnt_v, ipcw_v, ev_v, ord_v,
           later, earlier, eta_send, eta_recv, tot_send, tot_recv, res_send, res_all,
           core_send, core_recv, x_send, x_recv, y_send, y_recv,
           load_sem, eta_ss, eta_rs, tot_ss, tot_rs, res_ss, res_rs,
           core_ss, core_rs, x_ss, x_rs, y_ss, y_rs):
    s = lax.axis_index("samp")
    v = lax.axis_index("var")
    y, g = s // NG, s % NG
    x, c = g // NC, g % NC

    def zpeer(d):
        return (s, (v + d) % NZ)

    def gpeer(d):
        return (y * NG + (g + d) % NG, v)

    def ypeer(d):
        return (((y + d) % NY) * NG + g, v)

    def xpeer(d):
        return (y * NG + ((x + d) % NX) * NC + c, v)

    cpeer = (y * NG + x * NC + 1 - c, v)

    loads = [
        (order, ord_v), (beta, beta_v),
        (active.at[0:128], act_v.at[0:128]), (active.at[128:256], act_v.at[128:256]),
        (active.at[256:384], act_v.at[256:384]), (active.at[384:512], act_v.at[384:512]),
        (counts, cnt_v), (ipcw, ipcw_v), (events, ev_v), (screen, scr_v),
    ]
    loads = [pltpu.make_async_copy(a, b, load_sem.at[i]) for i, (a, b) in enumerate(loads)]
    for copy in loads:
        copy.start()

    barrier = pltpu.get_barrier_semaphore()
    for d in range(1, 8):
        for peer in (zpeer(d), gpeer(d), ypeer(d)):
            pl.semaphore_signal(barrier, inc=1, device_id=peer, device_id_type=MESH)

    def send(src, dst, ss, rs, peer):
        copy = pltpu.make_async_remote_copy(
            src_ref=src, dst_ref=dst, send_sem=ss, recv_sem=rs, device_id=peer, device_id_type=MESH)
        copy.start()
        return copy

    sent = []

    loads[0].wait()
    ranks = ord_v[...].astype(F32)
    for k in range(4):
        column = jnp.broadcast_to(ranks[:, k * 128:(k + 1) * 128], (128, 128)).T
        for j in range(4):
            line = jnp.broadcast_to(ranks[:, j * 128:(j + 1) * 128], (128, 128))
            later[k * 128:(k + 1) * 128, j * 128:(j + 1) * 128] = jnp.where(column >= line, 1.0, 0.0).astype(BF16)
            earlier[k * 128:(k + 1) * 128, j * 128:(j + 1) * 128] = jnp.where(column <= line, 1.0, 0.0).astype(BF16)

    loads[1].wait()
    coefs = beta_v[...]
    for k in range(4):
        loads[2 + k].wait()
        part = jnp.dot(act_v[k * 128:(k + 1) * 128, :], coefs, preferred_element_type=F32)
        part = part.T
        h, lanes = k // 2, slice((k % 2) * 128, (k % 2) * 128 + 128)
        for dest in range(NZ):
            eta_send[dest, 4 * h:4 * h + 4, lanes] = part[4 * dest:4 * dest + 4, :]
    pl.semaphore_wait(barrier, 21)
    for d in range(1, NZ):
        sent.append(send(eta_send.at[(v + d) % NZ], eta_recv.at[d - 1], eta_ss.at[d - 1], eta_rs.at[d - 1], zpeer(d)))
    etas = list(sent)

    for i in (6, 7, 8):
        loads[i].wait()
    tile = cnt_v[pl.ds(pl.multiple_of((v // 2) * 8, 8), 8), :].astype(F32)
    wts = fold_halves(tile[:, :HALF], tile[:, HALF:], v % 2 == 1)
    top = row_iota((8, HALF)) < 4

    def by_half(line):
        return jnp.where(top, jnp.broadcast_to(line[:, :HALF], (8, HALF)), jnp.broadcast_to(line[:, HALF:], (8, HALF)))

    wts = wts * by_half(ipcw_v[...])
    flagged = by_half(ev_v[...].astype(F32)) * wts

    eta = eta_send[v]
    for d in range(1, NZ):
        etas[d - 1].wait_recv()
        eta = eta + eta_recv[d - 1]
    risk = wts * jnp.exp(eta)

    def entering(total, n, reverse):
        base = 4 * n
        out = jnp.zeros((1, 128), F32)
        for step, (place, peer) in enumerate(((g, gpeer), (y, ypeer))):
            at = 2 * n + step
            tot_send[at] = total
            copies = []
            for d in range(1, 8):
                copies.append(send(tot_send.at[at], tot_recv.at[at, d - 1], tot_ss.at[at, d - 1], tot_rs.at[at, d - 1], peer(d)))
            sent.extend(copies)
            yield None
            for d in range(1, 8):
                copies[d - 1].wait_recv()
                got = tot_recv[at, d - 1]
                wanted = (d > place) if reverse else (d <= place)
                out = out + jnp.where(wanted, got, 0.0)
                total = total + got
        yield out

    walk = entering(to_lanes(risk), 0, True)
    next(walk)
    suffix = masked_sums(risk, later)
    next(walk)
    after = next(walk)
    haz = flagged / (suffix + to_rows(after))
    walk = entering(to_lanes(haz), 1, False)
    next(walk)
    prefix = masked_sums(haz, earlier)
    next(walk)
    before = next(walk)
    resid = flagged - risk * (prefix + to_rows(before))

    res_send[...] = resid
    copies = []
    for d in range(1, NZ):
        copies.append(send(res_send, res_all.at[v], res_ss.at[d - 1], res_rs.at[d - 1], zpeer(d)))
    sent.extend(copies)
    res_all[v] = resid
    for copy in copies:
        copy.wait_recv()
    lows, highs = [], []
    for u in range(4):
        one, two = res_all[2 * u], res_all[2 * u + 1]
        lows.append(jnp.where(top, one, swap4(two)))
        highs.append(jnp.where(top, swap4(one), two))
    low = jnp.concatenate(lows, axis=0).astype(BF16)
    high = jnp.concatenate(highs, axis=0).astype(BF16)
    lhs = jnp.concatenate([low, high], axis=1)

    loads[9].wait()
    lane = lane_iota((8, 128))
    first32 = (lane // 32) % 2 == 0
    first64 = lane < 64
    copies = []
    for k in range(NY):
        for a, geno in enumerate((act_v, scr_v)):
            block = jnp.dot(lhs, geno[:, k * 256:(k + 1) * 256], preferred_element_type=F32)
            for t in range(2):
                for p in range(2):
                    one = block[16 * p:16 * p + 8, t * 128:(t + 1) * 128]
                    two = block[16 * p + 8:16 * p + 16, t * 128:(t + 1) * 128]
                    core_send[0, k, a * 4 + t * 2 + p] = jnp.where(first32, one, pltpu.roll(two, 32, 1))
                    core_send[1, k, a * 4 + t * 2 + p] = jnp.where(first32, pltpu.roll(one, 96, 1), two)
        copies.append(send(core_send.at[1 - c, k], core_recv.at[k], core_ss.at[k], core_rs.at[k], cpeer))
    sent.extend(copies)
    for k in range(NY):
        copies[k].wait_recv()
        for a in range(2):
            for t in range(2):
                i = a * 4 + t * 2
                one = core_send[c, k, i] + core_recv[k, i]
                two = core_send[c, k, i + 1] + core_recv[k, i + 1]
                x_send[2 * t, k, a] = jnp.where(first64, one, pltpu.roll(two, 64, 1))
                x_send[2 * t + 1, k, a] = jnp.where(first64, pltpu.roll(one, 64, 1), two)
    copies = []
    for d in range(1, NX):
        copies.append(send(x_send.at[(x + d) % NX], x_recv.at[d - 1], x_ss.at[d - 1], x_rs.at[d - 1], xpeer(d)))
    sent.extend(copies)
    for copy in copies:
        copy.wait_recv()
    y_send[...] = x_send[x] + x_recv[0] + x_recv[1] + x_recv[2]
    copies = []
    for d in range(1, NY):
        copies.append(send(y_send.at[(y + d) % NY], y_recv.at[d - 1], y_ss.at[d - 1], y_rs.at[d - 1], ypeer(d)))
    sent.extend(copies)
    final = y_send[y]
    for d in range(1, NY):
        copies[d - 1].wait_recv()
        final = final + y_recv[d - 1]
    final = final * scale
    for a, out in enumerate((grad, score)):
        for q in range(4):
            turned = final[a] if q == 0 else pltpu.roll(final[a], 128 - 32 * q, 1)
            out[8 * q:8 * q + 8, :] = turned[:, :32]
    for copy in sent:
        copy.wait_send()


def per_device(active_geno, screen_geno, beta, counts, ipcw, events, order):
    rows, columns = active_geno.shape
    scale = float(rows * lax.axis_size("samp")) ** (-0.5)
    out = jax.ShapeDtypeStruct((32, 32), F32)
    dma = pltpu.SemaphoreType.DMA
    return pl.pallas_call(
        functools.partial(kernel, scale),
        out_shape=(out, out),
        in_specs=[pl.BlockSpec(memory_space=pl.ANY)] * 7,
        out_specs=[pl.BlockSpec(memory_space=pltpu.VMEM)] * 2,
        scratch_shapes=[
            pltpu.VMEM((rows, columns), BF16), pltpu.VMEM((rows, columns), BF16),
            pltpu.VMEM((columns, 32), BF16), pltpu.VMEM((32, rows), jnp.int32),
            pltpu.VMEM((1, rows), F32), pltpu.VMEM((1, rows), jnp.int32), pltpu.VMEM((1, rows), jnp.int32),
            pltpu.VMEM((rows, rows), BF16), pltpu.VMEM((rows, rows), BF16),
            pltpu.VMEM((NZ, 8, HALF), F32), pltpu.VMEM((NZ - 1, 8, HALF), F32),
            pltpu.VMEM((4, 1, 128), F32), pltpu.VMEM((4, 7, 1, 128), F32),
            pltpu.VMEM((8, HALF), F32), pltpu.VMEM((NZ, 8, HALF), F32),
            pltpu.VMEM((2, NY, 8, 8, 128), F32), pltpu.VMEM((NY, 8, 8, 128), F32),
            pltpu.VMEM((NX, NY, 2, 8, 128), F32), pltpu.VMEM((NX - 1, NY, 2, 8, 128), F32),
            pltpu.VMEM((NY, 2, 8, 128), F32), pltpu.VMEM((NY - 1, 2, 8, 128), F32),
            dma((10,)), dma((7,)), dma((7,)), dma((4, 7)), dma((4, 7)), dma((7,)), dma((7,)),
            dma((8,)), dma((8,)), dma((3,)), dma((3,)), dma((7,)), dma((7,)),
        ],
        compiler_params=pltpu.CompilerParams(
            collective_id=0, has_side_effects=True, vmem_limit_bytes=48 * 1024 * 1024),
    )(active_geno, screen_geno, beta, counts, ipcw.reshape(1, -1), events.reshape(1, -1), order)


def solution(mesh):
    placed = (
        P("samp", "var"),
        P("samp", "var"),
        P("var", None),
        P(None, "samp"),
        P("samp"),
        P("samp"),
        P("samp", None),
    )
    return jax.shard_map(
        per_device,
        mesh=mesh,
        in_specs=placed,
        out_specs=(P(None, ("var", "samp")), P(None, ("var", "samp"))),
        check_vma=False,
    )
```

time: 660 us -> 65.6 us (0.10)
  waiting for transfers between devices: 361 us -> 0 us
  blocking collectives: 257 us -> 0 us
  Pallas kernels: 0 us -> 56.1 us
  between operations: 14.6 us -> 0.66 us
  matrix products: 7.77 us -> 0 us
    unnamed x5 -> x0, waiting for transfers between devices: 284 us -> none
    unnamed x2 -> x0, blocking collectives: 257 us -> none
    psum x1 -> x0, waiting for transfers between devices: 76.4 us -> none  [per_device(): eta = lax.psum(partial_eta, 'var')]
    pallas_call x0 -> x1, Pallas kernels: none -> 56.1 us  [per_device(): pl.pallas_call(functools.partial(kernel, scale), out_shape=(out, out), in...]
    dot_general x5 -> x0, matrix products: 7.77 us -> none  [the longest x1 2.26 us: per_device(): lax.dot_general(beta, active_geno, (((0,), (1,)), ((), ())), preferred_el...]
  transfers between devices with their start and end apart: 3 -> 0, of which waited for: 3 -> 0; matrix products, arithmetic and copies ran while one was open for 1% -> 0% of each run, Pallas kernels for 0% -> 0%
where the time goes in v1:
time: 65.6 us; the launch traced here: 65.3 us
  Pallas kernels  56.1 us (86%)
  local copies, waits for them, and re-layouts  8.45 us (13%)
  between operations  0.66 us (1%)
    pallas_call x1, Pallas kernels, per_device(): pl.pallas_call(functools.partial(kernel, scale), out_shape=(out, out), in...  56.1 us
    unnamed x15, local copies, waits for them, and re-layouts  8.45 us

profile of v1, /device:TPU:1, one launch (start us, length us, event | category | flops | bytes accessed | tf_op | source)
XLA Modules:
  0.0 65.3 jit_solution(3403037835703977106)
XLA Ops:
  0.6 1.2 %copy.9.beta = bf16[2048,32]{1,0:T(8,128)(2,1)S(1)} copy(bf16[2048,32]{0,1:T(8,128)(2,1)} %param.9) | data formatting | bytes 262144 | tf_op args[2]
  1.8 0.0 copy-start
  1.8 1.6 %copy-done = bf16[512,2048]{1,0:T(8,128)(2,1)S(1)} copy-done((bf16[512,2048]{1,0:T(8,128)(2,1)S(1)}, bf16[512,2048]{1,0:T(8,128)(2,1)}, u32[]{:S(2)}) %copy-start) | copy-done | bytes 2097176
  3.4 0.0 copy-start.1
  3.4 1.6 %copy-done.1 = bf16[512,2048]{1,0:T(8,128)(2,1)S(1)} copy-done((bf16[512,2048]{1,0:T(8,128)(2,1)S(1)}, bf16[512,2048]{1,0:T(8,128)(2,1)}, u32[]{:S(2)}) %copy-start.1) | copy-done | bytes 2097176
  5.0 0.0 copy-start.2
  5.0 0.8 %copy-done.2 = s32[32,512]{1,0:T(8,128)S(1)} copy-done((s32[32,512]{1,0:T(8,128)S(1)}, s32[32,512]{1,0:T(8,128)}, u32[]{:S(2)}) %copy-start.2) | copy-done | bytes 65560
  5.8 0.0 copy-start.3
  5.8 0.7 %copy-done.3 = f32[512]{0:T(512)S(1)} copy-done((f32[512]{0:T(512)S(1)}, f32[512]{0:T(512)}, u32[]{:S(2)}) %copy-start.3) | copy-done | bytes 2072
  6.5 0.0 copy-start.4
  6.5 0.7 %copy-done.4 = s32[512]{0:T(512)S(1)} copy-done((s32[512]{0:T(512)S(1)}, s32[512]{0:T(512)}, u32[]{:S(2)}) %copy-start.4) | copy-done | bytes 2072
  7.2 0.0 copy-start.5
  7.2 0.7 %copy-done.5 = s32[1,512]{1,0:T(1,128)S(1)} copy-done((s32[1,512]{1,0:T(1,128)S(1)}, s32[1,512]{1,0:T(1,128)}, u32[]{:S(2)}) %copy-start.5) | copy-done | bytes 2072
  7.9 56.1 %shard_map.86 = (f32[32,32]{1,0:T(8,128)S(1)}, f32[32,32]{1,0:T(8,128)S(1)}) custom-call(bf16[512,2048]{1,0:T(8,128)(2,1)S(1)} %copy-done, bf16[512,2048]{1,0:T(8,128)(2,1)S(1)} %copy-done.1, bf16[2048,32]{1,0:T(8,128)(2,1)S(1)} %copy.9.beta, s32[32,512]{1,0:T(8,128)S(1)} %copy-done.2, f32[1,512]{1,0:T(1,128)S(1)} %bitcast.2, s32[1,512]{1,0:T(1,128)S(1)} %bitcast.3, ...), custom_call_target="tpu_custom_call" | custom-call | tf_op jit(solution)/shard_map/pallas_call | solution.py:261
  64.0 0.6 copy.12
  64.7 0.6 copy.13
Async XLA Ops:
  1.8 1.6 %copy-start = (bf16[512,2048]{1,0:T(8,128)(2,1)S(1)}, bf16[512,2048]{1,0:T(8,128)(2,1)}, u32[]{:S(2)}) copy-start(bf16[512,2048]{1,0:T(8,128)(2,1)} %active.1) | copy-start | bytes 6291460
  3.4 1.6 %copy-start.1 = (bf16[512,2048]{1,0:T(8,128)(2,1)S(1)}, bf16[512,2048]{1,0:T(8,128)(2,1)}, u32[]{:S(2)}) copy-start(bf16[512,2048]{1,0:T(8,128)(2,1)} %screen.1) | copy-start | bytes 6291460
  5.0 0.8 %copy-start.2 = (s32[32,512]{1,0:T(8,128)S(1)}, s32[32,512]{1,0:T(8,128)}, u32[]{:S(2)}) copy-start(s32[32,512]{1,0:T(8,128)} %counts.1) | copy-start | bytes 196612
  5.8 0.7 %copy-start.3 = (f32[512]{0:T(512)S(1)}, f32[512]{0:T(512)}, u32[]{:S(2)}) copy-start(f32[512]{0:T(512)} %param.11) | copy-start | bytes 6148
  6.5 0.7 %copy-start.4 = (s32[512]{0:T(512)S(1)}, s32[512]{0:T(512)}, u32[]{:S(2)}) copy-start(s32[512]{0:T(512)} %param.12) | copy-start | bytes 6148
  7.2 0.7 %copy-start.5 = (s32[1,512]{1,0:T(1,128)S(1)}, s32[1,512]{1,0:T(1,128)}, u32[]{:S(2)}) copy-start(s32[1,512]{1,0:T(1,128)} %order.1) | copy-start | bytes 6148

commit v2 on v0

v2 whole, which is shorter than its diff:
```python
import functools
import jax
import jax.numpy as jnp
from jax import lax
from jax.experimental import pallas as pl
from jax.experimental.pallas import tpu as pltpu
from jax.sharding import PartitionSpec as P

MESH = pl.DeviceIdType.MESH
NY, NX, NC, NZ = 8, 4, 2, 8
CHIPS = NY * NX
BOOT = 32
HALF = 256
PARTS = 4
F32 = jnp.float32
BF16 = jnp.bfloat16


def ring(d, n):
    return min(d, n - d)


ZOFF = sorted(range(1, NZ), key=lambda d: -ring(d, NZ))
YOFF = sorted(range(NY), key=lambda d: -ring(d, NY))
XOFF = sorted(range(1, NX), key=lambda d: -ring(d, NX))
CHIPOFF = sorted(
    [(dy, dx) for dy in range(NY) for dx in range(NX) if dy or dx],
    key=lambda o: -(ring(o[0], NY) + ring(o[1], NX)))


def lane_iota(shape):
    return lax.broadcasted_iota(jnp.int32, shape, 1)


def row_iota(shape):
    return lax.broadcasted_iota(jnp.int32, shape, 0)


def swap4(tile):
    return pltpu.roll(tile, 4, 0)


def split2(value):
    high = value.astype(BF16)
    rest = (value - high.astype(F32)).astype(BF16)
    return jnp.concatenate([high, rest], axis=0)


def to_lanes(total):
    full = jnp.broadcast_to(total, (BOOT, 128))
    same = lane_iota((BOOT, 128)) == row_iota((BOOT, 128))
    return jnp.sum(jnp.where(same, full, 0.0), axis=0, keepdims=True)


def to_rows(line):
    full = jnp.broadcast_to(line, (BOOT, 128))
    same = lane_iota((BOOT, 128)) == row_iota((BOOT, 128))
    return jnp.sum(jnp.where(same, full, 0.0), axis=1, keepdims=True)


def kernel(scale, active, screen, beta, counts, ipcw, events, order, grad, score,
           act_v, scr_v, beta_v, cnt_v, ipcw_v, ev_v, ord_v,
           later, earlier, eta_send, eta_recv, sum_send, eta_all,
           tot_own, tot_peer, tot_chip, tot_recv,
           two_send, two_recv, core_send, core_recv, x_send, x_recv, y_send, y_recv,
           load_sem, eta_ss, eta_rs, all_ss, all_rs, pair_ss, pair_rs, chip_ss, chip_rs,
           two_ss, two_rs, core_ss, core_rs, x_ss, x_rs, y_ss, y_rs):
    s = lax.axis_index("samp")
    v = lax.axis_index("var")
    y, g = s // (NX * NC), s % (NX * NC)
    x, c = g // NC, g % NC
    ybase = [((y + d) % NY) * (NX * NC) for d in range(NY)]
    xbase = [((x + d) % NX) * NC + c for d in range(NX)]
    chip = y * NX + x

    def zpeer(d):
        return (s, (v + d) % NZ)

    def chippeer(dy, dx):
        return (ybase[dy] + xbase[dx], v)

    cpeer = (y * (NX * NC) + x * NC + 1 - c, v)

    loads = [
        (order, ord_v), (beta, beta_v),
        (active.at[0:128], act_v.at[0:128]), (active.at[128:256], act_v.at[128:256]),
        (active.at[256:384], act_v.at[256:384]), (active.at[384:512], act_v.at[384:512]),
        (counts, cnt_v), (ipcw, ipcw_v), (events, ev_v), (screen, scr_v),
    ]
    loads = [pltpu.make_async_copy(a, b, load_sem.at[i]) for i, (a, b) in enumerate(loads)]
    for copy in loads:
        copy.start()

    barrier = pltpu.get_barrier_semaphore()

    def greet(peer):
        pl.semaphore_signal(barrier, inc=1, device_id=peer, device_id_type=MESH)

    for d in ZOFF:
        greet(zpeer(d))
    for dy, dx in CHIPOFF:
        greet(chippeer(dy, dx))
    greet(cpeer)

    def send(src, dst, ss, rs, peer):
        pltpu.make_async_remote_copy(
            src_ref=src, dst_ref=dst, send_sem=ss, recv_sem=rs, device_id=peer, device_id_type=MESH).start()

    def await_bytes(ref, sem):
        pltpu.make_async_copy(ref, ref, sem).wait()

    loads[1].wait()
    coefs = beta_v[...]
    for k in range(4):
        loads[2 + k].wait()
        part = lax.dot_general(
            coefs, act_v[k * 128:(k + 1) * 128, :], (((1,), (1,)), ((), ())), preferred_element_type=F32)
        h, lanes = k // 2, slice((k % 2) * 128, (k % 2) * 128 + 128)
        for dest in range(NZ):
            eta_send[dest, 4 * h:4 * h + 4, lanes] = part[4 * dest:4 * dest + 4, :]
    pl.semaphore_wait(barrier, NZ - 1 + CHIPS - 1 + 1)
    for d in ZOFF:
        send(eta_send.at[(v + d) % NZ], eta_recv.at[d - 1], eta_ss, eta_rs, zpeer(d))

    loads[0].wait()
    ranks = ord_v[...].astype(F32)
    for k in range(4):
        column = jnp.broadcast_to(ranks[:, k * 128:(k + 1) * 128], (128, 128)).T
        for j in range(4):
            line = jnp.broadcast_to(ranks[:, j * 128:(j + 1) * 128], (128, 128))
            later[k * 128:(k + 1) * 128, j * 128:(j + 1) * 128] = jnp.where(column >= line, 1.0, 0.0).astype(BF16)
            earlier[k * 128:(k + 1) * 128, j * 128:(j + 1) * 128] = jnp.where(column <= line, 1.0, 0.0).astype(BF16)
    for i in (6, 7, 8):
        loads[i].wait()
    wts = cnt_v[...].astype(F32) * ipcw_v[...]
    flagged = ev_v[...].astype(F32) * wts

    await_bytes(eta_recv, eta_rs)
    eta = eta_send[v]
    for d in range(1, NZ):
        eta = eta + eta_recv[d - 1]
    sum_send[...] = eta
    for d in ZOFF:
        send(sum_send, eta_all.at[v], all_ss, all_rs, zpeer(d))
    eta_all[v] = eta
    await_bytes(eta_all.at[0:NZ - 1], all_rs)
    top = row_iota((8, HALF)) < 4
    lows, highs = [], []
    for u in range(4):
        one, two = eta_all[2 * u], eta_all[2 * u + 1]
        lows.append(jnp.where(top, one, swap4(two)))
        highs.append(jnp.where(top, swap4(one), two))
    eta = jnp.concatenate([jnp.concatenate(lows, axis=0), jnp.concatenate(highs, axis=0)], axis=1)
    risk = wts * jnp.exp(eta)

    def pair_start(n, total):
        tot_own[n] = total
        send(tot_own.at[n], tot_peer.at[n], pair_ss.at[n], pair_rs.at[n], cpeer)

    def chip_start(n, total):
        await_bytes(tot_peer.at[n], pair_rs.at[n])
        peer = tot_peer[n]
        tot_chip[n] = total + peer
        for dy, dx in CHIPOFF:
            send(tot_chip.at[n], tot_recv.at[n, chip], chip_ss.at[n], chip_rs.at[n], chippeer(dy, dx))
        return peer

    def chip_end(n, wanted):
        await_bytes(tot_recv.at[n, 0:CHIPS - 1], chip_rs.at[n])
        out = jnp.zeros((1, 128), F32)
        for k in range(CHIPS):
            out = out + jnp.where(wanted(k), tot_recv[n, k], 0.0)
        return out

    lane = lane_iota((8, 128))
    first32 = (lane // 32) % 2 == 0
    first64 = lane < 64

    def project(pieces, j, out):
        place = pl.multiple_of(((y + YOFF[j]) % NY) * HALF, HALF)
        for a, geno in enumerate((act_v, scr_v)):
            block = jnp.dot(pieces, geno[:, pl.ds(place, HALF)], preferred_element_type=F32)
            block = block[:BOOT] + block[BOOT:]
            for t in range(2):
                for p in range(2):
                    one = block[16 * p:16 * p + 8, t * 128:(t + 1) * 128]
                    two = block[16 * p + 8:16 * p + 16, t * 128:(t + 1) * 128]
                    out[0, j, a * 4 + t * 2 + p] = jnp.where(first32, one, pltpu.roll(two, 32, 1))
                    out[1, j, a * 4 + t * 2 + p] = jnp.where(first32, pltpu.roll(one, 96, 1), two)

    total = to_lanes(jnp.sum(risk, axis=1, keepdims=True))
    pair_start(0, total)
    pieces = split2(risk)
    suffix = jnp.dot(pieces, later[...], preferred_element_type=F32)
    suffix = suffix[:BOOT] + suffix[BOOT:]
    peer = chip_start(0, total)
    loads[9].wait()
    for j in range(NY):
        project(pieces, j, two_send)
    send(two_send.at[1 - c], two_recv, two_ss, two_rs, cpeer)
    after = chip_end(0, lambda k: k > chip)
    after = after + jnp.where(c == 0, peer, 0.0)
    haz = flagged / (suffix + to_rows(after))

    total = to_lanes(jnp.sum(haz, axis=1, keepdims=True))
    pair_start(1, total)
    prefix = jnp.dot(split2(haz), earlier[...], preferred_element_type=F32)
    prefix = prefix[:BOOT] + prefix[BOOT:]
    peer = chip_start(1, total)
    pieces = split2(flagged - risk * prefix)
    for j in range(NY):
        project(pieces, j, core_send)
        send(core_send.at[1 - c, j], core_recv.at[j], core_ss.at[j], core_rs.at[j], cpeer)
    await_bytes(two_recv, two_rs)
    before = chip_end(1, lambda k: k < chip)

    def factors(line):
        rows = jnp.broadcast_to(to_rows(line), (BOOT, 128))
        return [jnp.where(first32, rows[16 * p:16 * p + 8], rows[16 * p + 8:16 * p + 16]) for p in range(2)]

    mine = factors(before + jnp.where(c == 1, peer, 0.0))
    other = factors(before + jnp.where(c == 0, total, 0.0))

    size = NY // PARTS
    for part in range(PARTS):
        for j in range(part * size, (part + 1) * size):
            await_bytes(core_recv.at[j], core_rs.at[j])
            for a in range(2):
                for t in range(2):
                    both = []
                    for p in range(2):
                        i = a * 4 + t * 2 + p
                        both.append(
                            core_send[c, j, i] + core_recv[j, i]
                            - (mine[p] * two_send[c, j, i] + other[p] * two_recv[j, i]))
                    one, two = both
                    x_send[2 * t, j, a] = jnp.where(first64, one, pltpu.roll(two, 64, 1))
                    x_send[2 * t + 1, j, a] = jnp.where(first64, pltpu.roll(one, 64, 1), two)
        piece = pl.ds(part * size, size)
        for d in XOFF:
            send(x_send.at[(x + d) % NX, piece], x_recv.at[part, d - 1], x_ss, x_rs.at[part], chippeer(0, d))
    for part in range(PARTS):
        await_bytes(x_recv.at[part], x_rs.at[part])
        for j in range(part * size, (part + 1) * size):
            i = j - part * size
            y_send[j] = (x_send[x, j] + x_recv[part, 0, i]) + (x_recv[part, 1, i] + x_recv[part, 2, i])
            if YOFF[j]:
                send(y_send.at[j], y_recv.at[j], y_ss, y_rs, chippeer(YOFF[j], 0))
    await_bytes(eta_recv, eta_ss)
    await_bytes(eta_all.at[0:NZ - 1], all_ss)
    for n in range(2):
        await_bytes(tot_peer.at[n], pair_ss.at[n])
        await_bytes(tot_recv.at[n, 0:CHIPS - 1], chip_ss.at[n])
    await_bytes(two_recv, two_ss)
    for j in range(NY):
        await_bytes(core_recv.at[j], core_ss.at[j])
    await_bytes(x_recv, x_ss)
    await_bytes(y_recv, y_rs)
    final = y_send[NY - 1]
    for j in range(NY - 1):
        final = final + y_recv[j]
    final = final * scale
    for a, out in enumerate((grad, score)):
        for q in range(4):
            turned = final[a] if q == 0 else pltpu.roll(final[a], 128 - 32 * q, 1)
            out[8 * q:8 * q + 8, :] = turned[:, :32]
    await_bytes(y_recv, y_ss)


def per_device(active_geno, screen_geno, beta, counts, ipcw, events, order):
    rows, columns = active_geno.shape
    scale = float(rows * lax.axis_size("samp")) ** (-0.5)
    out = jax.ShapeDtypeStruct((32, 32), F32)
    dma = pltpu.SemaphoreType.DMA
    return pl.pallas_call(
        functools.partial(kernel, scale),
        out_shape=(out, out),
        in_specs=[pl.BlockSpec(memory_space=pltpu.HBM)] * 7,
        out_specs=[pl.BlockSpec(memory_space=pltpu.VMEM)] * 2,
        scratch_shapes=[
            pltpu.VMEM((rows, columns), BF16), pltpu.VMEM((rows, columns), BF16),
            pltpu.VMEM((32, columns), BF16), pltpu.VMEM((32, rows), jnp.int32),
            pltpu.VMEM((1, rows), F32), pltpu.VMEM((1, rows), jnp.int32), pltpu.VMEM((1, rows), jnp.int32),
            pltpu.VMEM((rows, rows), BF16), pltpu.VMEM((rows, rows), BF16),
            pltpu.VMEM((NZ, 8, HALF), F32), pltpu.VMEM((NZ - 1, 8, HALF), F32),
            pltpu.VMEM((8, HALF), F32), pltpu.VMEM((NZ, 8, HALF), F32),
            pltpu.VMEM((2, 1, 128), F32), pltpu.VMEM((2, 1, 128), F32),
            pltpu.VMEM((2, 1, 128), F32), pltpu.VMEM((2, CHIPS, 1, 128), F32),
            pltpu.VMEM((2, NY, 8, 8, 128), F32), pltpu.VMEM((NY, 8, 8, 128), F32),
            pltpu.VMEM((2, NY, 8, 8, 128), F32), pltpu.VMEM((NY, 8, 8, 128), F32),
            pltpu.VMEM((NX, NY, 2, 8, 128), F32), pltpu.VMEM((PARTS, NX - 1, NY // PARTS, 2, 8, 128), F32),
            pltpu.VMEM((NY, 2, 8, 128), F32), pltpu.VMEM((NY - 1, 2, 8, 128), F32),
            dma((10,)), dma, dma, dma, dma, dma((2,)), dma((2,)), dma((2,)), dma((2,)),
            dma, dma, dma((NY,)), dma((NY,)), dma, dma((PARTS,)), dma, dma,
        ],
        compiler_params=pltpu.CompilerParams(
            collective_id=0, has_side_effects=True, vmem_limit_bytes=60 * 1024 * 1024),
    )(active_geno, screen_geno, beta.T, counts, ipcw.reshape(1, -1), events.reshape(1, -1), order)


def solution(mesh):
    placed = (
        P("samp", "var"),
        P("samp", "var"),
        P("var", None),
        P(None, "samp"),
        P("samp"),
        P("samp"),
        P("samp", None),
    )
    return jax.shard_map(
        per_device,
        mesh=mesh,
        in_specs=placed,
        out_specs=(P(None, ("var", "samp")), P(None, ("var", "samp"))),
        check_vma=False,
    )
```

time: 660 us -> 49.1 us (0.07)
  the two profiles are of different devices: /device:TPU:1 before, /device:TPU:8 now
where the time goes in v2:
time: 49.1 us; the launch traced here: 48.8 us
  Pallas kernels  45.6 us (93%)
  local copies, waits for them, and re-layouts  2.65 us (5%)
  between operations  0.64 us (1%)
    pallas_call x1, Pallas kernels, per_device(): pl.pallas_call(functools.partial(kernel, scale), out_shape=(out, out), in...  45.6 us
    unnamed x2, local copies, waits for them, and re-layouts  2.65 us

profile of v2, /device:TPU:8, one launch (start us, length us, event | category | flops | bytes accessed | tf_op | source)
XLA Modules:
  0.0 48.8 jit_solution(16426785487125772762)
XLA Ops:
  0.6 45.6 %shard_map.86 = (f32[32,32]{1,0:T(8,128)}, f32[32,32]{1,0:T(8,128)}) custom-call(bf16[512,2048]{1,0:T(8,128)(2,1)} %active.1, bf16[512,2048]{1,0:T(8,128)(2,1)} %screen.1, bf16[32,2048]{1,0:T(8,128)(2,1)} %bitcast.3, s32[32,512]{1,0:T(8,128)} %counts.1, f32[1,512]{1,0:T(1,128)} %bitcast.4, s32[1,512]{1,0:T(1,128)} %bitcast.5, s32[1,512]{1,0:T(1,128)} %order.1), custom_call_target="tpu_custom_call" | custom-call | tf_op jit(solution)/shard_map/pallas_call | solution.py:275
  46.2 1.3 %copy.11 = f32[32,32]{1,0:T(8,128)} copy(f32[32,32]{1,0:T(8,128)} %get-tuple-element.4) | data formatting | bytes 8192
  47.5 1.3 %copy.12 = f32[32,32]{1,0:T(8,128)} copy(f32[32,32]{1,0:T(8,128)} %get-tuple-element.5) | data formatting | bytes 8192

commit v3 on v2

--- a/solution.py
+++ b/solution.py
@@ -12,6 +12,7 @@
 BOOT = 32
 HALF = 256
 PARTS = 4
+LAG = 3
 F32 = jnp.float32
 BF16 = jnp.bfloat16
 
@@ -58,13 +59,13 @@
     return jnp.sum(jnp.where(same, full, 0.0), axis=1, keepdims=True)
 
 
-def kernel(scale, active, screen, beta, counts, ipcw, events, order, grad, score,
+def kernel(scale, active, screen, beta, counts, ipcw, events, order, result,
            act_v, scr_v, beta_v, cnt_v, ipcw_v, ev_v, ord_v,
            later, earlier, eta_send, eta_recv, sum_send, eta_all,
            tot_own, tot_peer, tot_chip, tot_recv,
-           two_send, two_recv, core_send, core_recv, x_send, x_recv, y_send, y_recv,
+           two_send, two_recv, core_send, core_recv, far_send, far_recv, x_send, x_recv, y_send, y_recv,
            load_sem, eta_ss, eta_rs, all_ss, all_rs, pair_ss, pair_rs, chip_ss, chip_rs,
-           two_ss, two_rs, core_ss, core_rs, x_ss, x_rs, y_ss, y_rs):
+           two_ss, two_rs, core_ss, core_rs, far_ss, far_rs, x_ss, x_rs, y_ss, y_rs):
     s = lax.axis_index("samp")
     v = lax.axis_index("var")
     y, g = s // (NX * NC), s % (NX * NC)
@@ -157,13 +158,15 @@
         tot_own[n] = total
         send(tot_own.at[n], tot_peer.at[n], pair_ss.at[n], pair_rs.at[n], cpeer)
 
-    def chip_start(n, total):
+    def pair_end(n, total):
         await_bytes(tot_peer.at[n], pair_rs.at[n])
         peer = tot_peer[n]
         tot_chip[n] = total + peer
-        for dy, dx in CHIPOFF:
+        return peer
+
+    def chip_send(n, offsets):
+        for dy, dx in offsets:
             send(tot_chip.at[n], tot_recv.at[n, chip], chip_ss.at[n], chip_rs.at[n], chippeer(dy, dx))
-        return peer
 
     def chip_end(n, wanted):
         await_bytes(tot_recv.at[n, 0:CHIPS - 1], chip_rs.at[n])
@@ -188,16 +191,32 @@
                     out[0, j, a * 4 + t * 2 + p] = jnp.where(first32, one, pltpu.roll(two, 32, 1))
                     out[1, j, a * 4 + t * 2 + p] = jnp.where(first32, pltpu.roll(one, 96, 1), two)
 
+    def spread(mine, theirs, j, out):
+        for a in range(2):
+            for t in range(2):
+                i = a * 4 + t * 2
+                one = mine[c, j, i] + theirs[j, i]
+                two = mine[c, j, i + 1] + theirs[j, i + 1]
+                out[2 * t, j, a] = jnp.where(first64, one, pltpu.roll(two, 64, 1))
+                out[2 * t + 1, j, a] = jnp.where(first64, pltpu.roll(one, 64, 1), two)
+
     total = to_lanes(jnp.sum(risk, axis=1, keepdims=True))
     pair_start(0, total)
     pieces = split2(risk)
+    peer = pair_end(0, total)
+    chip_send(0, CHIPOFF)
     suffix = jnp.dot(pieces, later[...], preferred_element_type=F32)
     suffix = suffix[:BOOT] + suffix[BOOT:]
-    peer = chip_start(0, total)
     loads[9].wait()
     for j in range(NY):
         project(pieces, j, two_send)
     send(two_send.at[1 - c], two_recv, two_ss, two_rs, cpeer)
+    await_bytes(two_recv, two_rs)
+    for j in range(NY):
+        spread(two_send, two_recv, j, far_send)
+    for d in XOFF:
+        send(far_send.at[(x + d) % NX], far_recv.at[d - 1], far_ss, far_rs, chippeer(0, d))
+
     after = chip_end(0, lambda k: k > chip)
     after = after + jnp.where(c == 0, peer, 0.0)
     haz = flagged / (suffix + to_rows(after))
@@ -206,44 +225,55 @@
     pair_start(1, total)
     prefix = jnp.dot(split2(haz), earlier[...], preferred_element_type=F32)
     prefix = prefix[:BOOT] + prefix[BOOT:]
-    peer = chip_start(1, total)
+    peer = pair_end(1, total)
+    prefix = prefix + to_rows(jnp.where(c == 1, peer, 0.0))
     pieces = split2(flagged - risk * prefix)
+
+    size = NY // PARTS
+
+    def to_x(j):
+        await_bytes(core_recv.at[j], core_rs.at[j])
+        spread(core_send, core_recv, j, x_send)
+        if (j + 1) % size == 0:
+            part = j // size
+            piece = pl.ds(part * size, size)
+            for d in XOFF:
+                send(x_send.at[(x + d) % NX, piece], x_recv.at[part, d - 1], x_ss, x_rs.at[part], chippeer(0, d))
+
     for j in range(NY):
         project(pieces, j, core_send)
         send(core_send.at[1 - c, j], core_recv.at[j], core_ss.at[j], core_rs.at[j], cpeer)
-    await_bytes(two_recv, two_rs)
-    before = chip_end(1, lambda k: k < chip)
-
-    def factors(line):
+        chip_send(1, CHIPOFF[4 * j:4 * j + 4])
+        if j >= LAG:
+            to_x(j - LAG)
+    for j in range(NY - LAG, NY):
+        to_x(j)
+
+    line = chip_end(1, lambda k: k < NX * y)
+    ahead = []
+    for k in range(NX):
+        ahead.append(line)
+        line = line + jnp.where(x == k, tot_chip[1], tot_recv[1, NX * y + k])
+    factors = []
+    for d in range(NX):
+        at = (x - d + NX) % NX
+        line = ahead[0]
+        for k in range(1, NX):
+            line = jnp.where(at == k, ahead[k], line)
         rows = jnp.broadcast_to(to_rows(line), (BOOT, 128))
-        return [jnp.where(first32, rows[16 * p:16 * p + 8], rows[16 * p + 8:16 * p + 16]) for p in range(2)]
-
-    mine = factors(before + jnp.where(c == 1, peer, 0.0))
-    other = factors(before + jnp.where(c == 0, total, 0.0))
-
-    size = NY // PARTS
-    for part in range(PARTS):
-        for j in range(part * size, (part + 1) * size):
-            await_bytes(core_recv.at[j], core_rs.at[j])
-            for a in range(2):
-                for t in range(2):
-                    both = []
-                    for p in range(2):
-                        i = a * 4 + t * 2 + p
-                        both.append(
-                            core_send[c, j, i] + core_recv[j, i]
-                            - (mine[p] * two_send[c, j, i] + other[p] * two_recv[j, i]))
-                    one, two = both
-                    x_send[2 * t, j, a] = jnp.where(first64, one, pltpu.roll(two, 64, 1))
-                    x_send[2 * t + 1, j, a] = jnp.where(first64, pltpu.roll(one, 64, 1), two)
-        piece = pl.ds(part * size, size)
-        for d in XOFF:
-            send(x_send.at[(x + d) % NX, piece], x_recv.at[part, d - 1], x_ss, x_rs.at[part], chippeer(0, d))
+        tile = rows[0:8]
+        for q in range(1, 4):
+            tile = jnp.where(lane // 32 == q, rows[8 * q:8 * q + 8], tile)
+        factors.append(tile)
+    await_bytes(far_recv, far_rs)
     for part in range(PARTS):
         await_bytes(x_recv.at[part], x_rs.at[part])
         for j in range(part * size, (part + 1) * size):
             i = j - part * size
-            y_send[j] = (x_send[x, j] + x_recv[part, 0, i]) + (x_recv[part, 1, i] + x_recv[part, 2, i])
+            less = factors[0] * far_send[x, j] + factors[1] * far_recv[0, j]
+            less = less + (factors[2] * far_recv[1, j] + factors[3] * far_recv[2, j])
+            full = (x_send[x, j] + x_recv[part, 0, i]) + (x_recv[part, 1, i] + x_recv[part, 2, i])
+            y_send[j] = full - less
             if YOFF[j]:
                 send(y_send.at[j], y_recv.at[j], y_ss, y_rs, chippeer(YOFF[j], 0))
     await_bytes(eta_recv, eta_ss)
@@ -255,28 +285,29 @@
     for j in range(NY):
         await_bytes(core_recv.at[j], core_ss.at[j])
     await_bytes(x_recv, x_ss)
+    await_bytes(far_recv, far_ss)
     await_bytes(y_recv, y_rs)
     final = y_send[NY - 1]
     for j in range(NY - 1):
         final = final + y_recv[j]
     final = final * scale
-    for a, out in enumerate((grad, score)):
+    for a in range(2):
         for q in range(4):
             turned = final[a] if q == 0 else pltpu.roll(final[a], 128 - 32 * q, 1)
-            out[8 * q:8 * q + 8, :] = turned[:, :32]
+            result[a, 8 * q:8 * q + 8, :] = turned[:, :32]
     await_bytes(y_recv, y_ss)
 
 
 def per_device(active_geno, screen_geno, beta, counts, ipcw, events, order):
     rows, columns = active_geno.shape
     scale = float(rows * lax.axis_size("samp")) ** (-0.5)
-    out = jax.ShapeDtypeStruct((32, 32), F32)
+    out = jax.ShapeDtypeStruct((2, BOOT, 32), F32)
     dma = pltpu.SemaphoreType.DMA
-    return pl.pallas_call(
+    result = pl.pallas_call(
         functools.partial(kernel, scale),
-        out_shape=(out, out),
+        out_shape=out,
         in_specs=[pl.BlockSpec(memory_space=pltpu.HBM)] * 7,
-        out_specs=[pl.BlockSpec(memory_space=pltpu.VMEM)] * 2,
+        out_specs=pl.BlockSpec(memory_space=pltpu.VMEM),
         scratch_shapes=[
             pltpu.VMEM((rows, columns), BF16), pltpu.VMEM((rows, columns), BF16),
             pltpu.VMEM((32, columns), BF16), pltpu.VMEM((32, rows), jnp.int32),
@@ -288,14 +319,16 @@
             pltpu.VMEM((2, 1, 128), F32), pltpu.VMEM((2, CHIPS, 1, 128), F32),
             pltpu.VMEM((2, NY, 8, 8, 128), F32), pltpu.VMEM((NY, 8, 8, 128), F32),
             pltpu.VMEM((2, NY, 8, 8, 128), F32), pltpu.VMEM((NY, 8, 8, 128), F32),
+            pltpu.VMEM((NX, NY, 2, 8, 128), F32), pltpu.VMEM((NX - 1, NY, 2, 8, 128), F32),
             pltpu.VMEM((NX, NY, 2, 8, 128), F32), pltpu.VMEM((PARTS, NX - 1, NY // PARTS, 2, 8, 128), F32),
             pltpu.VMEM((NY, 2, 8, 128), F32), pltpu.VMEM((NY - 1, 2, 8, 128), F32),
             dma((10,)), dma, dma, dma, dma, dma((2,)), dma((2,)), dma((2,)), dma((2,)),
-            dma, dma, dma((NY,)), dma((NY,)), dma, dma((PARTS,)), dma, dma,
+            dma, dma, dma((NY,)), dma((NY,)), dma, dma, dma, dma((PARTS,)), dma, dma,
         ],
         compiler_params=pltpu.CompilerParams(
             collective_id=0, has_side_effects=True, vmem_limit_bytes=60 * 1024 * 1024),
     )(active_geno, screen_geno, beta.T, counts, ipcw.reshape(1, -1), events.reshape(1, -1), order)
+    return result[0], result[1]
 
 
 def solution(mesh):

time: 49.1 us -> 45 us (0.916)
  the two profiles are of different devices: /device:TPU:8 before, /device:TPU:1 now
where the time goes in v3:
time: 45 us; the launch traced here: 44.8 us
  Pallas kernels  42.8 us (95%)
  local copies, waits for them, and re-layouts  1.35 us (3%)
  between operations  0.64 us (1%)
    pallas_call x1, Pallas kernels, per_device(): pl.pallas_call(functools.partial(kernel, scale), out_shape=out, in_specs=...  42.8 us
    squeeze x1, local copies, waits for them, and re-layouts, per_device(): return (result[0], result[1])  1.35 us

profile of v3, /device:TPU:1, one launch (start us, length us, event | category | flops | bytes accessed | tf_op | source)
XLA Modules:
  0.0 44.8 jit_solution(2443831292781091816)
XLA Ops:
  0.6 42.8 %shard_map.86 = f32[2,32,32]{2,1,0:T(8,128)} custom-call(bf16[512,2048]{1,0:T(8,128)(2,1)} %active.1, bf16[512,2048]{1,0:T(8,128)(2,1)} %screen.1, bf16[32,2048]{1,0:T(8,128)(2,1)} %bitcast.7, s32[32,512]{1,0:T(8,128)} %counts.1, f32[1,512]{1,0:T(1,128)} %bitcast.8, s32[1,512]{1,0:T(1,128)} %bitcast.9, s32[1,512]{1,0:T(1,128)} %order.1), custom_call_target="tpu_custom_call" | custom-call | tf_op jit(solution)/shard_map/pallas_call | solution.py:306
  43.5 1.3 %slice_bitcast_fusion = (f32[32,32]{1,0:T(8,128)}, f32[32,32]{1,0:T(8,128)}) fusion(f32[2,32,32]{2,1,0:T(8,128)} %shard_map.86), kind=kLoop, calls=%fused_computation | loop fusion | bytes 16384 | tf_op jit(solution)/shard_map/squeeze | solution.py:331

commit v4 on v3

--- a/solution.py
+++ b/solution.py
@@ -62,10 +62,10 @@
 def kernel(scale, active, screen, beta, counts, ipcw, events, order, result,
            act_v, scr_v, beta_v, cnt_v, ipcw_v, ev_v, ord_v,
            later, earlier, eta_send, eta_recv, sum_send, eta_all,
-           tot_own, tot_peer, tot_chip, tot_recv,
+           risk_own, risk_all, tot_own, tot_peer, tot_chip, tot_recv,
            two_send, two_recv, core_send, core_recv, far_send, far_recv, x_send, x_recv, y_send, y_recv,
-           load_sem, eta_ss, eta_rs, all_ss, all_rs, pair_ss, pair_rs, chip_ss, chip_rs,
-           two_ss, two_rs, core_ss, core_rs, far_ss, far_rs, x_ss, x_rs, y_ss, y_rs):
+           load_sem, eta_ss, eta_rs, all_ss, all_rs, risk_ss, risk_rs, pair_ss, pair_rs, chip_ss, chip_rs,
+           two_ss, two_rs, core_ss, core_rs, far_ss, far_rs, x_ss, x_rs, y_ss, y_rs, ready):
     s = lax.axis_index("samp")
     v = lax.axis_index("var")
     y, g = s // (NX * NC), s % (NX * NC)
@@ -80,7 +80,26 @@
     def chippeer(dy, dx):
         return (ybase[dy] + xbase[dx], v)
 
+    def otherpeer(dy, dx):
+        return (ybase[dy] + xbase[dx] + (1 - 2 * c), v)
+
     cpeer = (y * (NX * NC) + x * NC + 1 - c, v)
+
+    barrier = pltpu.get_barrier_semaphore()
+
+    def greet(peer):
+        pl.semaphore_signal(barrier, inc=1, device_id=peer, device_id_type=MESH)
+
+    for hops in range(NY // 2 + NX // 2, 0, -1):
+        for dy, dx in CHIPOFF:
+            if (dy == 0 or dx == 0) and ring(dy, NY) + ring(dx, NX) == hops:
+                greet(chippeer(dy, dx))
+                if dy == 0:
+                    greet(otherpeer(dy, dx))
+        for d in ZOFF:
+            if ring(d, NZ) == hops:
+                greet(zpeer(d))
+    greet(cpeer)
 
     loads = [
         (order, ord_v), (beta, beta_v),
@@ -92,17 +111,6 @@
     for copy in loads:
         copy.start()
 
-    barrier = pltpu.get_barrier_semaphore()
-
-    def greet(peer):
-        pl.semaphore_signal(barrier, inc=1, device_id=peer, device_id_type=MESH)
-
-    for d in ZOFF:
-        greet(zpeer(d))
-    for dy, dx in CHIPOFF:
-        greet(chippeer(dy, dx))
-    greet(cpeer)
-
     def send(src, dst, ss, rs, peer):
         pltpu.make_async_remote_copy(
             src_ref=src, dst_ref=dst, send_sem=ss, recv_sem=rs, device_id=peer, device_id_type=MESH).start()
@@ -119,9 +127,12 @@
         h, lanes = k // 2, slice((k % 2) * 128, (k % 2) * 128 + 128)
         for dest in range(NZ):
             eta_send[dest, 4 * h:4 * h + 4, lanes] = part[4 * dest:4 * dest + 4, :]
-    pl.semaphore_wait(barrier, NZ - 1 + CHIPS - 1 + 1)
+    pl.semaphore_wait(barrier, NZ - 1 + NY - 1 + NX * NC - 1)
     for d in ZOFF:
         send(eta_send.at[(v + d) % NZ], eta_recv.at[d - 1], eta_ss, eta_rs, zpeer(d))
+
+    for d in YOFF[:NY - 1]:
+        pl.semaphore_signal(ready, inc=1, device_id=chippeer(d, 0), device_id_type=MESH)
 
     loads[0].wait()
     ranks = ord_v[...].astype(F32)
@@ -154,25 +165,25 @@
     eta = jnp.concatenate([jnp.concatenate(lows, axis=0), jnp.concatenate(highs, axis=0)], axis=1)
     risk = wts * jnp.exp(eta)
 
-    def pair_start(n, total):
-        tot_own[n] = total
-        send(tot_own.at[n], tot_peer.at[n], pair_ss.at[n], pair_rs.at[n], cpeer)
-
-    def pair_end(n, total):
-        await_bytes(tot_peer.at[n], pair_rs.at[n])
-        peer = tot_peer[n]
-        tot_chip[n] = total + peer
+    def pair_start(total):
+        tot_own[...] = total
+        send(tot_own, tot_peer, pair_ss, pair_rs, cpeer)
+
+    def pair_end(total):
+        await_bytes(tot_peer, pair_rs)
+        peer = tot_peer[...]
+        tot_chip[...] = total + peer
         return peer
 
-    def chip_send(n, offsets):
+    def chip_send(offsets):
         for dy, dx in offsets:
-            send(tot_chip.at[n], tot_recv.at[n, chip], chip_ss.at[n], chip_rs.at[n], chippeer(dy, dx))
-
-    def chip_end(n, wanted):
-        await_bytes(tot_recv.at[n, 0:CHIPS - 1], chip_rs.at[n])
+            send(tot_chip, tot_recv.at[chip], chip_ss, chip_rs, chippeer(dy, dx))
+
+    def chip_end(wanted):
+        await_bytes(tot_recv.at[0:CHIPS - 1], chip_rs)
         out = jnp.zeros((1, 128), F32)
         for k in range(CHIPS):
-            out = out + jnp.where(wanted(k), tot_recv[n, k], 0.0)
+            out = out + jnp.where(wanted(k), tot_recv[k], 0.0)
         return out
 
     lane = lane_iota((8, 128))
@@ -201,10 +212,13 @@
                 out[2 * t + 1, j, a] = jnp.where(first64, pltpu.roll(one, 64, 1), two)
 
     total = to_lanes(jnp.sum(risk, axis=1, keepdims=True))
-    pair_start(0, total)
+    pl.semaphore_wait(ready, NY - 1)
+    risk_own[...] = total
+    for dy, dx in CHIPOFF:
+        for peer in (chippeer(dy, dx), otherpeer(dy, dx)):
+            send(risk_own, risk_all.at[s], risk_ss, risk_rs, peer)
+    send(risk_own, risk_all.at[s], risk_ss, risk_rs, cpeer)
     pieces = split2(risk)
-    peer = pair_end(0, total)
-    chip_send(0, CHIPOFF)
     suffix = jnp.dot(pieces, later[...], preferred_element_type=F32)
     suffix = suffix[:BOOT] + suffix[BOOT:]
     loads[9].wait()
@@ -217,15 +231,17 @@
     for d in XOFF:
         send(far_send.at[(x + d) % NX], far_recv.at[d - 1], far_ss, far_rs, chippeer(0, d))
 
-    after = chip_end(0, lambda k: k > chip)
-    after = after + jnp.where(c == 0, peer, 0.0)
+    await_bytes(risk_all.at[0:2 * CHIPS - 1], risk_rs)
+    after = jnp.zeros((1, 128), F32)
+    for k in range(2 * CHIPS):
+        after = after + jnp.where(k > s, risk_all[k], 0.0)
     haz = flagged / (suffix + to_rows(after))
 
     total = to_lanes(jnp.sum(haz, axis=1, keepdims=True))
-    pair_start(1, total)
+    pair_start(total)
     prefix = jnp.dot(split2(haz), earlier[...], preferred_element_type=F32)
     prefix = prefix[:BOOT] + prefix[BOOT:]
-    peer = pair_end(1, total)
+    peer = pair_end(total)
     prefix = prefix + to_rows(jnp.where(c == 1, peer, 0.0))
     pieces = split2(flagged - risk * prefix)
 
@@ -243,17 +259,17 @@
     for j in range(NY):
         project(pieces, j, core_send)
         send(core_send.at[1 - c, j], core_recv.at[j], core_ss.at[j], core_rs.at[j], cpeer)
-        chip_send(1, CHIPOFF[4 * j:4 * j + 4])
+        chip_send(CHIPOFF[4 * j:4 * j + 4])
         if j >= LAG:
             to_x(j - LAG)
     for j in range(NY - LAG, NY):
         to_x(j)
 
-    line = chip_end(1, lambda k: k < NX * y)
+    line = chip_end(lambda k: k < NX * y)
     ahead = []
     for k in range(NX):
         ahead.append(line)
-        line = line + jnp.where(x == k, tot_chip[1], tot_recv[1, NX * y + k])
+        line = line + jnp.where(x == k, tot_chip[...], tot_recv[NX * y + k])
     factors = []
     for d in range(NX):
         at = (x - d + NX) % NX
@@ -278,9 +294,9 @@
                 send(y_send.at[j], y_recv.at[j], y_ss, y_rs, chippeer(YOFF[j], 0))
     await_bytes(eta_recv, eta_ss)
     await_bytes(eta_all.at[0:NZ - 1], all_ss)
-    for n in range(2):
-        await_bytes(tot_peer.at[n], pair_ss.at[n])
-        await_bytes(tot_recv.at[n, 0:CHIPS - 1], chip_ss.at[n])
+    await_bytes(risk_all.at[0:2 * CHIPS - 1], risk_ss)
+    await_bytes(tot_peer, pair_ss)
+    await_bytes(tot_recv.at[0:CHIPS - 1], chip_ss)
     await_bytes(two_recv, two_ss)
     for j in range(NY):
         await_bytes(core_recv.at[j], core_ss.at[j])
@@ -315,15 +331,16 @@
             pltpu.VMEM((rows, rows), BF16), pltpu.VMEM((rows, rows), BF16),
             pltpu.VMEM((NZ, 8, HALF), F32), pltpu.VMEM((NZ - 1, 8, HALF), F32),
             pltpu.VMEM((8, HALF), F32), pltpu.VMEM((NZ, 8, HALF), F32),
-            pltpu.VMEM((2, 1, 128), F32), pltpu.VMEM((2, 1, 128), F32),
-            pltpu.VMEM((2, 1, 128), F32), pltpu.VMEM((2, CHIPS, 1, 128), F32),
+            pltpu.VMEM((1, 128), F32), pltpu.VMEM((2 * CHIPS, 1, 128), F32),
+            pltpu.VMEM((1, 128), F32), pltpu.VMEM((1, 128), F32),
+            pltpu.VMEM((1, 128), F32), pltpu.VMEM((CHIPS, 1, 128), F32),
             pltpu.VMEM((2, NY, 8, 8, 128), F32), pltpu.VMEM((NY, 8, 8, 128), F32),
             pltpu.VMEM((2, NY, 8, 8, 128), F32), pltpu.VMEM((NY, 8, 8, 128), F32),
             pltpu.VMEM((NX, NY, 2, 8, 128), F32), pltpu.VMEM((NX - 1, NY, 2, 8, 128), F32),
             pltpu.VMEM((NX, NY, 2, 8, 128), F32), pltpu.VMEM((PARTS, NX - 1, NY // PARTS, 2, 8, 128), F32),
             pltpu.VMEM((NY, 2, 8, 128), F32), pltpu.VMEM((NY - 1, 2, 8, 128), F32),
-            dma((10,)), dma, dma, dma, dma, dma((2,)), dma((2,)), dma((2,)), dma((2,)),
-            dma, dma, dma((NY,)), dma((NY,)), dma, dma, dma, dma((PARTS,)), dma, dma,
+            dma((10,)), dma, dma, dma, dma, dma, dma, dma, dma, dma, dma,
+            dma, dma, dma((NY,)), dma((NY,)), dma, dma, dma, dma((PARTS,)), dma, dma, pltpu.SemaphoreType.REGULAR,
         ],
         compiler_params=pltpu.CompilerParams(
             collective_id=0, has_side_effects=True, vmem_limit_bytes=60 * 1024 * 1024),

time: 45 us -> 44 us (0.978)
  Pallas kernels: 42.8 us -> 41.8 us
    pallas_call x1, Pallas kernels: 42.8 us -> 41.8 us  [per_device(): pl.pallas_call(functools.partial(kernel, scale), out_shape=out, in_specs=...]
where the time goes in v4:
time: 44 us; the launch traced here: 43.8 us
  Pallas kernels  41.8 us (95%)
  local copies, waits for them, and re-layouts  1.35 us (3%)
  between operations  0.64 us (1%)
    pallas_call x1, Pallas kernels, per_device(): pl.pallas_call(functools.partial(kernel, scale), out_shape=out, in_specs=...  41.8 us
    squeeze x1, local copies, waits for them, and re-layouts, per_device(): return (result[0], result[1])  1.35 us

profile of v4, /device:TPU:1, one launch (start us, length us, event | category | flops | bytes accessed | tf_op | source)
XLA Modules:
  0.0 43.8 jit_solution(18408566567555725339)
XLA Ops:
  0.6 41.8 %shard_map.86 = f32[2,32,32]{2,1,0:T(8,128)} custom-call(bf16[512,2048]{1,0:T(8,128)(2,1)} %active.1, bf16[512,2048]{1,0:T(8,128)(2,1)} %screen.1, bf16[32,2048]{1,0:T(8,128)(2,1)} %bitcast.7, s32[32,512]{1,0:T(8,128)} %counts.1, f32[1,512]{1,0:T(1,128)} %bitcast.8, s32[1,512]{1,0:T(1,128)} %bitcast.9, s32[1,512]{1,0:T(1,128)} %order.1), custom_call_target="tpu_custom_call" | custom-call | tf_op jit(solution)/shard_map/pallas_call | solution.py:322
  42.4 1.3 %slice_bitcast_fusion = (f32[32,32]{1,0:T(8,128)}, f32[32,32]{1,0:T(8,128)}) fusion(f32[2,32,32]{2,1,0:T(8,128)} %shard_map.86), kind=kLoop, calls=%fused_computation | loop fusion | bytes 16384 | tf_op jit(solution)/shard_map/squeeze | solution.py:348

commit v5 on v4

--- a/solution.py
+++ b/solution.py
@@ -241,14 +241,15 @@
     pair_start(total)
     prefix = jnp.dot(split2(haz), earlier[...], preferred_element_type=F32)
     prefix = prefix[:BOOT] + prefix[BOOT:]
-    peer = pair_end(total)
-    prefix = prefix + to_rows(jnp.where(c == 1, peer, 0.0))
     pieces = split2(flagged - risk * prefix)
 
     size = NY // PARTS
 
-    def to_x(j):
+    def to_x(j, factors):
         await_bytes(core_recv.at[j], core_rs.at[j])
+        for i in range(8):
+            less = factors[0][i % 2] * two_send[c, j, i] + factors[1][i % 2] * two_recv[j, i]
+            core_recv[j, i] = core_recv[j, i] - less
         spread(core_send, core_recv, j, x_send)
         if (j + 1) % size == 0:
             part = j // size
@@ -256,14 +257,23 @@
             for d in XOFF:
                 send(x_send.at[(x + d) % NX, piece], x_recv.at[part, d - 1], x_ss, x_rs.at[part], chippeer(0, d))
 
+    def by_core(line):
+        rows = jnp.broadcast_to(to_rows(line), (BOOT, 128))
+        return [jnp.where(first32, rows[16 * p:16 * p + 8], rows[16 * p + 8:16 * p + 16]) for p in range(2)]
+
+    factors = None
     for j in range(NY):
         project(pieces, j, core_send)
         send(core_send.at[1 - c, j], core_recv.at[j], core_ss.at[j], core_rs.at[j], cpeer)
-        chip_send(CHIPOFF[4 * j:4 * j + 4])
+        if j == 1:
+            peer = pair_end(total)
+            factors = by_core(jnp.where(c == 1, peer, 0.0)), by_core(jnp.where(c == 0, total, 0.0))
+        if j >= 1:
+            chip_send(CHIPOFF[5 * (j - 1):5 * j])
         if j >= LAG:
-            to_x(j - LAG)
+            to_x(j - LAG, factors)
     for j in range(NY - LAG, NY):
-        to_x(j)
+        to_x(j, factors)
 
     line = chip_end(lambda k: k < NX * y)
     ahead = []

time: 44 us -> 43.5 us (0.989)
  Pallas kernels: 41.8 us -> 41.3 us
where the time goes in v5:
time: 43.5 us; the launch traced here: 43.3 us
  Pallas kernels  41.3 us (95%)
  local copies, waits for them, and re-layouts  1.35 us (3%)
  between operations  0.64 us (1%)
    pallas_call x1, Pallas kernels, per_device(): pl.pallas_call(functools.partial(kernel, scale), out_shape=out, in_specs=...  41.3 us
    squeeze x1, local copies, waits for them, and re-layouts, per_device(): return (result[0], result[1])  1.35 us

profile of v5, /device:TPU:1, one launch (start us, length us, event | category | flops | bytes accessed | tf_op | source)
XLA Modules:
  0.0 43.3 jit_solution(449551405062290082)
XLA Ops:
  0.6 41.3 %shard_map.86 = f32[2,32,32]{2,1,0:T(8,128)} custom-call(bf16[512,2048]{1,0:T(8,128)(2,1)} %active.1, bf16[512,2048]{1,0:T(8,128)(2,1)} %screen.1, bf16[32,2048]{1,0:T(8,128)(2,1)} %bitcast.7, s32[32,512]{1,0:T(8,128)} %counts.1, f32[1,512]{1,0:T(1,128)} %bitcast.8, s32[1,512]{1,0:T(1,128)} %bitcast.9, s32[1,512]{1,0:T(1,128)} %order.1), custom_call_target="tpu_custom_call" | custom-call | tf_op jit(solution)/shard_map/pallas_call | solution.py:332
  42.0 1.3 %slice_bitcast_fusion = (f32[32,32]{1,0:T(8,128)}, f32[32,32]{1,0:T(8,128)}) fusion(f32[2,32,32]{2,1,0:T(8,128)} %shard_map.86), kind=kLoop, calls=%fused_computation | loop fusion | bytes 16384 | tf_op jit(solution)/shard_map/squeeze | solution.py:358

commit v6 on v5

--- a/solution.py
+++ b/solution.py
@@ -232,9 +232,10 @@
         send(far_send.at[(x + d) % NX], far_recv.at[d - 1], far_ss, far_rs, chippeer(0, d))
 
     await_bytes(risk_all.at[0:2 * CHIPS - 1], risk_rs)
-    after = jnp.zeros((1, 128), F32)
+    chains = [jnp.zeros((1, 128), F32) for _ in range(4)]
     for k in range(2 * CHIPS):
-        after = after + jnp.where(k > s, risk_all[k], 0.0)
+        chains[k % 4] = chains[k % 4] + jnp.where(k > s, risk_all[k], 0.0)
+    after = (chains[0] + chains[1]) + (chains[2] + chains[3])
     haz = flagged / (suffix + to_rows(after))
 
     total = to_lanes(jnp.sum(haz, axis=1, keepdims=True))

time: 43.5 us -> 43.5 us (level)
  no operation moved by 1% of the time
where the time goes in v6:
time: 43.5 us; the launch traced here: 43.3 us
  Pallas kernels  41.3 us (95%)
  local copies, waits for them, and re-layouts  1.35 us (3%)
  between operations  0.64 us (1%)
    pallas_call x1, Pallas kernels, per_device(): pl.pallas_call(functools.partial(kernel, scale), out_shape=out, in_specs=...  41.3 us
    squeeze x1, local copies, waits for them, and re-layouts, per_device(): return (result[0], result[1])  1.35 us

profile of v6, /device:TPU:1, one launch (start us, length us, event | category | flops | bytes accessed | tf_op | source)
XLA Modules:
  0.0 43.3 jit_solution(5276536169607082680)
XLA Ops:
  0.6 41.3 %shard_map.86 = f32[2,32,32]{2,1,0:T(8,128)} custom-call(bf16[512,2048]{1,0:T(8,128)(2,1)} %active.1, bf16[512,2048]{1,0:T(8,128)(2,1)} %screen.1, bf16[32,2048]{1,0:T(8,128)(2,1)} %bitcast.7, s32[32,512]{1,0:T(8,128)} %counts.1, f32[1,512]{1,0:T(1,128)} %bitcast.8, s32[1,512]{1,0:T(1,128)} %bitcast.9, s32[1,512]{1,0:T(1,128)} %order.1), custom_call_target="tpu_custom_call" | custom-call | tf_op jit(solution)/shard_map/pallas_call | solution.py:333
  42.0 1.3 %slice_bitcast_fusion = (f32[32,32]{1,0:T(8,128)}, f32[32,32]{1,0:T(8,128)}) fusion(f32[2,32,32]{2,1,0:T(8,128)} %shard_map.86), kind=kLoop, calls=%fused_computation | loop fusion | bytes 16384 | tf_op jit(solution)/shard_map/squeeze | solution.py:359
